TPU v7x, 32 devices: a whole 2x2x4 slice. The times are simulated.
32 devices in a mesh: row: 4 (over y, core), col: 8 (over z, x).
Axes of the slice: x: 2, y: 2, z: 4, core: 2. Of those that a mesh axis runs over, the one named last changes fastest.
Arguments:
- seq_ids: int32 [1024], replicated, may hold values from 0 to 3, never falling along the last dimension, each value on 1 to 512 neighbouring positions
- query_inputs: bfloat16 [1024, 8192], P('col', 'row'), may hold values from -6 to 6
- query_grads: bfloat16 [1024, 8192], P('row', 'col'), may hold values from -0.25 to 0.25
- query_act_basis: bfloat16 [8192, 8192], P('row', 'col'), may hold values from -0.0625 to 0.0625
- query_grad_basis: bfloat16 [8192, 8192], P('col', 'row'), may hold values from -0.0625 to 0.0625
- output_inputs: bfloat16 [1024, 8192], P('col', 'row'), may hold values from -6 to 6
- output_grads: bfloat16 [1024, 8192], P('row', 'col'), may hold values from -0.25 to 0.25
- output_act_basis: bfloat16 [8192, 8192], P('row', 'col'), may hold values from -0.0625 to 0.0625
- output_grad_basis: bfloat16 [8192, 8192], P('col', 'row'), may hold values from -0.0625 to 0.0625
Outputs:
- query_corr: float32 [8192, 8192], P('row', 'col')
- output_corr: float32 [8192, 8192], P('row', 'col')
Inputs may be any that keep to these rules, and one draw needn't show every extreme that they name: seq_ids never falls along the tokens; each of the 4 sequences holds 1 to 512 tokens, and one holds exactly 512.
All inputs are finite; a program needn't handle non-finite values.
Results may differ from a plain program's by a relative error of at most 0.0003.
Values may be sent and summed in bfloat16 or wider, within the bound.
A program may use at most 128 MiB of HBM per device.

v0:
```python
import jax
import jax.numpy as jnp
from jax import lax
from jax.sharding import PartitionSpec as P

SEQS = 4
MOST = 512


def gather_act(inputs_now):
    return lax.all_gather(inputs_now, "col", axis=0, tiled=True)


def gather_grad(grads_now):
    return lax.all_gather(grads_now, "row", axis=0, tiled=True)


def reduce_act(partial_value):
    return lax.psum(partial_value, "row")


def reduce_grad(partial_value):
    return lax.psum(partial_value, "col")


def correct(act_rot, grad_rot, seq_ids):
    numbers = jnp.arange(SEQS, dtype=jnp.int32)
    counts = jnp.sum((seq_ids[None, :] == numbers[:, None]).astype(jnp.int32), axis=1)
    starts = jnp.cumsum(counts) - counts
    padded_act = jnp.concatenate([act_rot, jnp.zeros((MOST, act_rot.shape[1]), act_rot.dtype)], 0)
    padded_grad = jnp.concatenate(
        [grad_rot, jnp.zeros((MOST, grad_rot.shape[1]), grad_rot.dtype)], 0
    )
    offsets = jnp.arange(MOST, dtype=jnp.int32)
    running = jnp.zeros((grad_rot.shape[1], act_rot.shape[1]), jnp.float32)
    for seq_index in range(SEQS):
        act_rows = lax.dynamic_slice_in_dim(padded_act, starts[seq_index], MOST, 0)
        grad_rows = lax.dynamic_slice_in_dim(padded_grad, starts[seq_index], MOST, 0)
        inside = offsets < counts[seq_index]
        grad_rows = jnp.where(inside[:, None], grad_rows, jnp.zeros_like(grad_rows))
        product = lax.dot_general(
            grad_rows, act_rows, (((0,), (0,)), ((), ())), precision=lax.Precision.HIGHEST
        )
        running = running + product * product
    return running / SEQS


def act_term(gathered_act, act_eigen):
    return jnp.dot(gathered_act, act_eigen, preferred_element_type=jnp.float32)


def grad_term(gathered_grad, grad_eigen):
    return jnp.dot(gathered_grad, grad_eigen, preferred_element_type=jnp.float32)


def finish(seq_ids, gathered_act, gathered_grad, act_eigen, grad_eigen):
    act_rot = reduce_act(act_term(gathered_act, act_eigen))
    grad_rot = reduce_grad(grad_term(gathered_grad, grad_eigen))
    return correct(act_rot, grad_rot, seq_ids)


def per_device(
    seq_ids,
    query_inputs,
    query_grads,
    query_act_basis,
    query_grad_basis,
    output_inputs,
    output_grads,
    output_act_basis,
    output_grad_basis,
):
    projections = (
        (query_inputs, query_grads, query_act_basis, query_grad_basis),
        (output_inputs, output_grads, output_act_basis, output_grad_basis),
    )
    results = []
    for inputs_now, grads_now, act_eigen, grad_eigen in projections:
        results.append(
            finish(seq_ids, gather_act(inputs_now), gather_grad(grads_now), act_eigen, grad_eigen)
        )
    return (results[0], results[1])


def solution(mesh):
    in_specs = (
        P(),
        P("col", "row"),
        P("row", "col"),
        P("row", "col"),
        P("col", "row"),
        P("col", "row"),
        P("row", "col"),
        P("row", "col"),
        P("col", "row"),
    )
    out_specs = (P("row", "col"), P("row", "col"))
    return jax.shard_map(
        per_device, mesh=mesh, in_specs=in_specs, out_specs=out_specs, check_vma=False
    )
```

profile of v0, /device:TPU:24, one launch (start us, length us, event | category | flops | bytes accessed | tf_op | source)
XLA Modules:
  0.0 1027.2 jit_solution(9271405374956260458)
XLA Ops:
  7.2 0.0 all-gather.7.cloned.1.call-start
  7.2 0.7 all-gather.7.cloned.1.call-update
  7.9 0.0 all-gather.11.cloned.1.call-start
  7.9 0.7 all-gather.11.cloned.1.call-update
  8.6 0.0 all-gather.5.cloned.1.call-start
  8.7 0.7 all-gather.5.cloned.1.call-update
  9.4 0.0 all-gather.9.cloned.1.call-start
  9.4 0.5 all-gather.9.cloned.1.call-update
  10.0 0.0 all-reduce.11.cloned.1.call-start
  10.0 72.8 %all-gather.7.cloned.1.call-done = bf16[1024,2048]{1,0:T(8,128)(2,1)} async-done(((bf16[128,2048]{1,0:T(8,128)(2,1)}), bf16[1024,2048]{1,0:T(8,128)(2,1)}) %all-gather.7.cloned.1.call-update) | async-done | bytes 4194320 | tf_op jit(solution)/shard_map/all_gather | solution.py:11
  82.8 9.9 fusion.57
  92.7 63.9 %all-gather.11.cloned.1.call-done = bf16[1024,2048]{1,0:T(8,128)(2,1)} async-done(((bf16[128,2048]{1,0:T(8,128)(2,1)}), bf16[1024,2048]{1,0:T(8,128)(2,1)}) %all-gather.11.cloned.1.call-update) | async-done | bytes 4194320 | tf_op jit(solution)/shard_map/all_gather | solution.py:11
  156.6 9.9 fusion.59
  166.5 0.0 all-reduce.11.cloned.1.call-update
  166.5 0.3 all-reduce.9.cloned.1.call-start
  166.8 14.0 %all-gather.5.cloned.1.call-done = bf16[1024,1024]{1,0:T(8,128)(2,1)} async-done(((bf16[256,1024]{1,0:T(8,128)(2,1)}), bf16[1024,1024]{1,0:T(8,128)(2,1)}) %all-gather.5.cloned.1.call-update) | async-done | bytes 2097168 | tf_op jit(solution)/shard_map/all_gather | solution.py:15
  180.8 10.7 %fusion.56 = f32[1024,2048]{1,0:T(8,128)} fusion(bf16[1024,1024]{1,0:T(8,128)(2,1)} %all-gather.5.cloned.1.call-done, bf16[1024,2048]{1,0:T(8,128)(2,1)} %param.13), kind=kOutput, calls=%fused_computation.73 | convolution fusion | flops 4294967296 | bytes 14680064 | tf_op jit(solution)/shard_map/dot_general | solution.py:53
  191.5 13.3 %all-gather.9.cloned.1.call-done = bf16[1024,1024]{1,0:T(8,128)(2,1)} async-done(((bf16[256,1024]{1,0:T(8,128)(2,1)}), bf16[1024,1024]{1,0:T(8,128)(2,1)}) %all-gather.9.cloned.1.call-update) | async-done | bytes 2097168 | tf_op jit(solution)/shard_map/all_gather | solution.py:15
  204.8 10.8 %fusion.58 = f32[1024,2048]{1,0:T(8,128)} fusion(bf16[1024,1024]{1,0:T(8,128)(2,1)} %all-gather.9.cloned.1.call-done, bf16[1024,2048]{1,0:T(8,128)(2,1)} %param.17), kind=kOutput, calls=%fused_computation.75 | convolution fusion | flops 4294967296 | bytes 14680064 | tf_op jit(solution)/shard_map/dot_general | solution.py:53
  215.7 0.0 copy-start.3
  215.7 0.0 all-reduce.9.cloned.1.call-update
  215.7 0.7 copy-done.3
  216.4 0.1 convert_reduce_fusion
  216.5 0.2 reduce-window.9
  216.7 0.7 fusion.55
  224.9 0.7 fusion.54
  225.5 0.7 iota_compare_fusion.4
  226.2 0.7 iota_compare_fusion.3
  226.9 0.5 iota_compare_fusion.2
  227.5 0.6 iota_compare_fusion.1
  228.1 132.4 %all-reduce.11.cloned.1.call-done = (f32[1024,1024]{1,0:T(8,128)}, f32[1024,1024]{1,0:T(8,128)}) async-done(((f32[1024,1024]{1,0:T(8,128)}, f32[1024,1024]{1,0:T(8,128)}), (f32[1024,1024]{1,0:T(8,128)}, f32[1024,1024]{1,0:T(8,128)})) %all-reduce.11.cloned.1.call-update) | async-done | bytes 8388624 | tf_op jit(solution)/shard_map/psum | solution.py:19
  360.6 512.8 %all-reduce.9.cloned.1.call-done = (f32[1024,2048]{1,0:T(8,128)}, f32[1024,2048]{1,0:T(8,128)}) async-done(((f32[1024,2048]{1,0:T(8,128)}, f32[1024,2048]{1,0:T(8,128)}), (f32[1024,2048]{1,0:T(8,128)}, f32[1024,2048]{1,0:T(8,128)})) %all-reduce.9.cloned.1.call-update) | async-done | bytes 16777232 | tf_op jit(solution)/shard_map/psum | solution.py:23
  873.4 0.0 copy-start
  873.4 0.0 copy-start.2
  873.4 18.6 %fusion.12 = f32[2048,1024]{1,0:T(8,128)} fusion(s32[]{:T(128)S(6)} %select_n.49, f32[1024,2048]{1,0:T(8,128)} %get-tuple-element.3, f32[1024,1024]{1,0:T(8,128)} %get-tuple-element.5, pred[512]{0:T(512)(128)(4,1)S(1)} %iota_compare_fusion.4), kind=kOutput, calls=%fused_computation.26 | convolution fusion | flops 12885950464 | bytes 20973056 | tf_op jit(solution)/shard_map/dot_general | solution.py:41
  892.0 0.0 copy-done
  892.0 0.0 copy-done.2
  892.0 0.0 copy-start.1
  892.0 16.7 %fusion.15 = f32[2048,1024]{1,0:T(8,128)} fusion(s32[]{:T(128)S(6)} %select_n.51, f32[1024,2048]{1,0:T(8,128)S(1)} %copy-done, f32[1024,1024]{1,0:T(8,128)S(1)} %copy-done.2, pred[512]{0:T(512)(128)(4,1)S(1)} %iota_compare_fusion.3), kind=kOutput, calls=%fused_computation.28 | convolution fusion | flops 12885950464 | bytes 20973056 | tf_op jit(solution)/shard_map/dot_general | solution.py:41
  908.8 0.0 slice-done
  908.8 0.0 slice-done.1
  908.8 0.0 copy-done.1
  908.8 16.8 %fusion.1 = f32[2048,1024]{1,0:T(8,128)} fusion(s32[]{:T(128)S(6)} %select_n.49, f32[1024,2048]{1,0:T(8,128)S(1)} %bitcast.20, f32[1024,1024]{1,0:T(8,128)S(1)} %copy-done.1, pred[512]{0:T(512)(128)(4,1)S(1)} %iota_compare_fusion.4), kind=kOutput, calls=%fused_computation.19 | convolution fusion | flops 12885950464 | bytes 20973056 | tf_op jit(solution)/shard_map/dot_general | solution.py:41
  925.6 16.4 %fusion.4 = f32[2048,1024]{1,0:T(8,128)} fusion(s32[]{:T(128)S(6)} %select_n.51, f32[1024,2048]{1,0:T(8,128)S(1)} %bitcast.20, f32[1024,1024]{1,0:T(8,128)S(1)} %copy-done.1, pred[512]{0:T(512)(128)(4,1)S(1)} %iota_compare_fusion.3), kind=kOutput, calls=%fused_computation.21 | convolution fusion | flops 12885950464 | bytes 20973056 | tf_op jit(solution)/shard_map/dot_general | solution.py:41
  942.0 16.6 %fusion.18 = f32[2048,1024]{1,0:T(8,128)} fusion(s32[]{:T(128)S(6)} %select_n.53, f32[1024,2048]{1,0:T(8,128)S(1)} %copy-done, f32[1024,1024]{1,0:T(8,128)S(1)} %copy-done.2, pred[512]{0:T(512)(128)(4,1)S(1)} %iota_compare_fusion.2), kind=kOutput, calls=%fused_computation.30 | convolution fusion | flops 12885950464 | bytes 20973056 | tf_op jit(solution)/shard_map/dot_general | solution.py:41
  958.5 16.6 %fusion.7 = f32[2048,1024]{1,0:T(8,128)} fusion(s32[]{:T(128)S(6)} %select_n.53, f32[1024,2048]{1,0:T(8,128)S(1)} %bitcast.20, f32[1024,1024]{1,0:T(8,128)S(1)} %copy-done.1, pred[512]{0:T(512)(128)(4,1)S(1)} %iota_compare_fusion.2), kind=kOutput, calls=%fused_computation.23 | convolution fusion | flops 12885950464 | bytes 20973056 | tf_op jit(solution)/shard_map/dot_general | solution.py:41
  975.1 23.4 %add_multiply_fusion = f32[2048,1024]{1,0:T(8,128)} fusion(f32[2048,1024]{1,0:T(8,128)} %fusion.18, f32[2048,1024]{1,0:T(8,128)} %fusion.15, f32[2048,1024]{1,0:T(8,128)} %fusion.12, s32[]{:T(128)S(6)} %select_n.55, f32[1024,2048]{1,0:T(8,128)} %get-tuple-element.3, f32[1024,1024]{1,0:T(8,128)} %get-tuple-element.5, pred[512]{0:T(512)(128)(4,1)S(1)} %iota_compare_fusion.1), kind=kOutput, calls=%fused_computation.8 | convolution fusion | flops 12902727680 | bytes 46138880 | tf_op jit(solution)/shard_map/dot_general | solution.py:41
  998.5 21.3 %add_multiply_fusion.1 = f32[2048,1024]{1,0:T(8,128)} fusion(f32[2048,1024]{1,0:T(8,128)} %fusion.7, f32[2048,1024]{1,0:T(8,128)} %fusion.4, f32[2048,1024]{1,0:T(8,128)} %fusion.1, s32[]{:T(128)S(6)} %select_n.55, f32[1024,2048]{1,0:T(8,128)S(1)} %bitcast.20, f32[1024,1024]{1,0:T(8,128)S(1)} %copy-done.1, pred[512]{0:T(512)(128)(4,1)S(1)} %iota_compare_fusion.1), kind=kOutput, calls=%fused_computation.9 | convolution fusion | flops 12902727680 | bytes 46138880 | tf_op jit(solution)/shard_map/dot_general | solution.py:41
  (4 shorter events, 0.0 us)
Async XLA Ops:
  7.2 75.6 %all-gather.7.cloned.1.call-start = ((), (), s32[]{:S(2)}) async-start(), calls=%async_computation.1 | async-start | bytes 4718592 | tf_op jit(solution)/shard_map/all_gather | solution.py:11
  7.9 148.7 %all-gather.11.cloned.1.call-start = ((), (), s32[]{:S(2)}) async-start(), calls=%async_computation.3 | async-start | bytes 4718592 | tf_op jit(solution)/shard_map/all_gather | solution.py:11
  8.6 172.2 %all-gather.5.cloned.1.call-start = ((), (), s32[]{:S(2)}) async-start(), calls=%async_computation | async-start | bytes 2621440 | tf_op jit(solution)/shard_map/all_gather | solution.py:15
  9.4 195.5 %all-gather.9.cloned.1.call-start = ((), (), s32[]{:S(2)}) async-start(), calls=%async_computation.2 | async-start | bytes 2621440 | tf_op jit(solution)/shard_map/all_gather | solution.py:15
  10.0 350.6 %all-reduce.11.cloned.1.call-start = ((), (), s32[]{:S(2)}) async-start(), calls=%async_computation.5 | async-start | bytes 16777216 | tf_op jit(solution)/shard_map/psum | solution.py:19
  166.5 706.9 %all-reduce.9.cloned.1.call-start = ((), (), s32[]{:S(2)}) async-start(), calls=%async_computation.4 | async-start | bytes 33554432 | tf_op jit(solution)/shard_map/psum | solution.py:23
  215.7 0.7 copy-start.3
  873.4 18.6 %copy-start = (f32[1024,2048]{1,0:T(8,128)S(1)}, f32[1024,2048]{1,0:T(8,128)}, u32[]{:S(2)}) copy-start(f32[1024,2048]{1,0:T(8,128)} %get-tuple-element.3) | copy-start | bytes 25165828
  873.4 18.6 %copy-start.2 = (f32[1024,1024]{1,0:T(8,128)S(1)}, f32[1024,1024]{1,0:T(8,128)}, u32[]{:S(2)}) copy-start(f32[1024,1024]{1,0:T(8,128)} %get-tuple-element.5) | copy-start | bytes 12582916
  873.4 35.4 %slice-start = ((s8[8388608]{0:T(1024)(128)(4,1)}), s8[4194304]{0:T(1024)(128)(4,1)S(1)}, s32[]{:S(2)}) async-start(s8[8388608]{0:T(1024)(128)(4,1)} %bitcast.19), calls=%async_computation.6 | async-start | bytes 8388608
  892.0 16.7 %slice-start.1 = ((s8[8388608]{0:T(1024)(128)(4,1)}), s8[4194304]{0:T(1024)(128)(4,1)S(1)}, s32[]{:S(2)}) async-start(s8[8388608]{0:T(1024)(128)(4,1)} %bitcast.19), calls=%async_computation.7 | async-start | bytes 8388608
  892.0 16.7 %copy-start.1 = (f32[1024,1024]{1,0:T(8,128)S(1)}, f32[1024,1024]{1,0:T(8,128)}, u32[]{:S(2)}) copy-start(f32[1024,1024]{1,0:T(8,128)} %get-tuple-element.4) | copy-start | bytes 12582916
Sparse Core Ops, SparseCore 0:
  10.1 72.5 all-gather.6
  84.9 71.6 all-gather.10
  158.2 22.6 all-gather.4
  182.2 22.5 all-gather.8
  207.3 153.2 all-reduce.10
  365.3 508.0 all-reduce.8
where the time goes:
time: 1040 us; the launch traced here: 1030 us
  waiting for transfers between devices  812 us (78%)
  matrix products  188 us (18%)
  between operations  22.3 us (2%)
    psum x1, waiting for transfers between devices, reduce_grad(): return lax.psum(partial_value, 'col')  513 us
    dot_general x8, matrix products, correct(): lax.dot_general(grad_rows, act_rows, (((0,), (0,)), ((), ())), precision=...  146 us
    all_gather x2, waiting for transfers between devices, gather_act(): return lax.all_gather(inputs_now, 'col', axis=0, tiled=True)  137 us
    psum x1, waiting for transfers between devices, reduce_act(): return lax.psum(partial_value, 'row')  132 us
    all_gather x2, waiting for transfers between devices, gather_grad(): return lax.all_gather(grads_now, 'row', axis=0, tiled=True)  27.4 us
    dot_general x2, matrix products, grad_term(): jnp.dot(gathered_grad, grad_eigen, preferred_element_type=jnp.float32)  21.5 us
  transfers between devices with their start and end apart: 6, of which 6 were waited for; matrix products, arithmetic and copies ran while one was open for 4% of the time, Pallas kernels for 0%

commit v1 on v0

v1 whole, which is shorter than its diff:
```python
import functools

import jax
import jax.numpy as jnp
from jax import lax
from jax.experimental import pallas as pl
from jax.experimental.pallas import tpu as pltpu
from jax.sharding import PartitionSpec as P

SEQS = 4
CHUNK = 16
TOP = 32767.0
MESH = pl.DeviceIdType.MESH
F32, BF16, I16, I32 = jnp.float32, jnp.bfloat16, jnp.int16, jnp.int32


def quantize(load, store, store_scale, chunks, width):
    most = lax.fori_loop(
        0, chunks, lambda i, m: jnp.maximum(m, jnp.abs(load(i))), jnp.zeros((CHUNK, width), F32)
    )
    most = jnp.max(jnp.max(most, axis=1, keepdims=True), axis=0, keepdims=True)
    inverse = jnp.where(most > 1e-30, TOP / jnp.maximum(most, 1e-30), 0.0)
    store_scale(jnp.broadcast_to(most * (1.0 / TOP), (8, 128)))

    def body(i, carry):
        store(i, jnp.round(load(i) * inverse).astype(I32).astype(I16))
        return carry

    lax.fori_loop(0, chunks, body, 0)


def widen(codes, scale):
    return codes.astype(I32).astype(F32) * scale


def rows_of(i, size):
    return pl.ds(pl.multiple_of(i * size, size), size)


def rotate_kernel(n_row, n_col, *refs):
    ins, refs = (refs[0:4], refs[4:8]), refs[8:]
    outs, refs = (refs[0:4], refs[4:8]), refs[8:]
    (grads_all, inputs_all, basis_g, basis_a, block, own, xsend, xsend_s, xrecv, xrecv_s, zrecv, zrecv_s,
     fin, fin_s, aown, asend, asend_s, arecv, arecv_s, afin, afin_s,
     g_send, g_recv, i_send, f_send, i_recv, xs_send, xs_recv, zs_send, zs_recv,
     ag_send, agf_send, ag_recv, as_send, as_recv, aa_send, aa_recv, local) = refs

    r, c = lax.axis_index("row"), lax.axis_index("col")
    nz = n_col // 2
    z, x = c // 2, lax.rem(c, 2)
    partner = (r, z * 2 + 1 - x)
    tokens, feats_g = grads_all.shape[1:]
    feats_a = inputs_all.shape[2]
    width_g, width_a = basis_g.shape[2], basis_a.shape[2]
    t_col, t_row = tokens // n_col, tokens // n_row

    def zpeer(k):
        return (r, lax.rem(z + k, nz) * 2 + x)

    def rpeer(k):
        return (lax.rem(r + k, n_row), c)

    def rdma(src, dst, send, recv, device):
        return pltpu.make_async_remote_copy(
            src_ref=src, dst_ref=dst, send_sem=send, recv_sem=recv, device_id=device, device_id_type=MESH
        )

    class pair:
        def __init__(self, src, src_s, dst, dst_s, send, recv, device):
            self.both = (
                rdma(src, dst, send.at[0], recv.at[0], device),
                rdma(src_s, dst_s, send.at[1], recv.at[1], device),
            )

        def start(self):
            for one in self.both:
                one.start()

        def wait_send(self):
            for one in self.both:
                one.wait_send()

        def wait_recv(self):
            for one in self.both:
                one.wait_recv()

    def each(low, high, body):
        lax.fori_loop(low, high, lambda i, carry: (body(i), carry)[1], 0)

    barrier = pltpu.get_barrier_semaphore()

    def greet(device):
        pl.semaphore_signal(barrier, inc=1, device_id=device, device_id_type=MESH)

    greet(partner)
    each(1, nz, lambda k: greet(zpeer(k)))
    each(1, n_row, lambda k: greet(rpeer(k)))
    pl.semaphore_wait(barrier, 1 + (nz - 1) + (n_row - 1))

    def load(p, kind):
        if kind == "g":
            return pltpu.make_async_copy(ins[p][3], basis_g.at[p], local.at[p, 0])
        if kind == "a":
            return pltpu.make_async_copy(ins[p][2], basis_a.at[0], local.at[p, 1])
        if kind == "inputs":
            return pltpu.make_async_copy(ins[p][0], inputs_all.at[p, rows_of(c, t_col)], local.at[p, 2])
        return pltpu.make_async_copy(ins[p][1], grads_all.at[p, rows_of(r, t_row)], local.at[p, 3])

    def grads_copy(p, k, source):
        return rdma(ins[p][1], grads_all.at[p, rows_of(source, t_row)], g_send.at[p, k], g_recv.at[p, source], rpeer(k))

    def inputs_copy(p, k, source, device):
        return rdma(ins[p][0], inputs_all.at[p, rows_of(source, t_col)], i_send.at[p, k], i_recv.at[p, source], device)

    def inputs_forward(p, k, source):
        there = inputs_all.at[p, rows_of(source, t_col)]
        return rdma(there, there, f_send.at[p, k], i_recv.at[p, source], partner)

    for p in (0, 1):
        load(p, "grads").start()
        each(1, n_row, lambda k: grads_copy(p, k, r).start())
        load(p, "g").start()
        load(p, "inputs").start()
    for p in (0, 1):
        inputs_copy(p, 0, c, partner).start()
        each(1, nz, lambda k: inputs_copy(p, k, c, zpeer(k)).start())
    load(0, "a").start()

    def xcopy(p, zz):
        return pair(xsend.at[p, zz], xsend_s.at[p, zz], xrecv.at[p, zz], xrecv_s.at[p, zz],
                    xs_send.at[p, zz], xs_recv.at[p, zz], partner)

    def zcopy(p, k, slot, source):
        return pair(xrecv.at[p, slot], xrecv_s.at[p, slot], zrecv.at[p, source], zrecv_s.at[p, source],
                    zs_send.at[p, k], zs_recv.at[p, source], zpeer(k))

    def gather_copy(p, k, source, device):
        return pair(fin.at[p], fin_s.at[p], outs[p][0].at[source], outs[p][1].at[source],
                    ag_send.at[p, k], ag_recv.at[p, source], device)

    def gather_forward(p, k, source):
        return pair(outs[p][0].at[source], outs[p][1].at[source], outs[p][0].at[source], outs[p][1].at[source],
                    agf_send.at[p, k], ag_recv.at[p, source], partner)

    def acopy(p, k, slot, source):
        return pair(asend.at[p, slot], asend_s.at[p, slot], arecv.at[p, source], arecv_s.at[p, source],
                    as_send.at[p, k], as_recv.at[p, source], rpeer(k))

    def act_gather(p, k, source):
        return pair(afin.at[p], afin_s.at[p], outs[p][2].at[source], outs[p][3].at[source],
                    aa_send.at[p, k], aa_recv.at[p, source], rpeer(k))

    def put(ref, *at):
        def store(value):
            ref[at] = value

        return store

    def rotate_grads(p):
        load(p, "grads").wait()
        load(p, "g").wait()
        each(1, n_row, lambda k: grads_copy(p, k, lax.rem(r + n_row - k, n_row)).wait_recv())
        tile = min(512, width_g)

        def step(k):
            zz = lax.rem(z + k, nz)

            def columns(j):
                at = rows_of(j, tile)
                block[:, at] = jnp.dot(
                    grads_all[p, rows_of(zz, 2 * t_col), :], basis_g[p, :, at], preferred_element_type=F32
                )

            each(0, width_g // tile, columns)
            there, here = (1 - x) * (t_col // CHUNK), x * (t_col // CHUNK)

            def store(i, value):
                xsend[p, zz, rows_of(i, CHUNK), :] = value

            quantize(lambda i: block[rows_of(there + i, CHUNK), :], store, put(xsend_s, p, zz),
                     t_col // CHUNK, width_g)
            xcopy(p, zz).start()

            def keep(i):
                own[p, zz, rows_of(i, CHUNK), :] = block[rows_of(here + i, CHUNK), :]

            each(0, t_col // CHUNK, keep)

        each(0, nz, step)

    def forward_inputs(p):
        def step(k):
            source = lax.rem(z + nz - k, nz) * 2 + x
            inputs_copy(p, k, source, partner).wait_recv()
            inputs_forward(p, k, source).start()

        each(1, nz, step)

    def add_scaled(target, codes, scale, chunks):
        def step(i):
            at = rows_of(i, CHUNK)
            target[at, :] = target[at, :] + widen(codes[at, :], scale)

        each(0, chunks, step)

    def sum_x(p):
        chunks = t_col // CHUNK

        def step(k):
            zz = lax.rem(z + k, nz)
            xcopy(p, zz).wait_recv()
            add_scaled(own.at[p, zz], xrecv.at[p, zz], xrecv_s[p, zz, 0:1, 0:1], chunks)

            def store(i, value):
                xrecv[p, zz, rows_of(i, CHUNK), :] = value

            quantize(lambda i: own[p, zz, rows_of(i, CHUNK), :], store, put(xrecv_s, p, zz), chunks, width_g)
            zcopy(p, k, zz, z).start()

        each(1, nz, step)
        xcopy(p, z).wait_recv()
        add_scaled(own.at[p, z], xrecv.at[p, z], xrecv_s[p, z, 0:1, 0:1], chunks)

    def sum_z(p):
        chunks = t_col // CHUNK

        def step(k):
            source = lax.rem(z + nz - k, nz)
            zcopy(p, k, z, source).wait_recv()
            add_scaled(own.at[p, z], zrecv.at[p, source], zrecv_s[p, source, 0:1, 0:1], chunks)

        each(1, nz, step)

        def store(i, value):
            fin[p, rows_of(i, CHUNK), :] = value

        quantize(lambda i: own[p, z, rows_of(i, CHUNK), :], store, put(fin_s, p), chunks, width_g)
        gather_copy(p, 0, c, partner).start()
        each(1, nz, lambda k: gather_copy(p, k, c, zpeer(k)).start())
        pltpu.make_async_copy(fin.at[p], outs[p][0].at[c], local.at[p, 4]).start()
        pltpu.make_async_copy(fin_s.at[p], outs[p][1].at[c], local.at[p, 5]).start()

    def forward_gather(p):
        def step(k):
            source = lax.rem(z + nz - k, nz) * 2 + x
            gather_copy(p, k, source, partner).wait_recv()
            gather_forward(p, k, source).start()

        each(1, nz, step)

    def rotate_acts(p):
        load(p, "inputs").wait()
        load(p, "a").wait()
        inputs_copy(p, 0, z * 2 + 1 - x, partner).wait_recv()
        each(1, nz, lambda k: inputs_forward(p, k, lax.rem(z + nz - k, nz) * 2 + 1 - x).wait_recv())
        tile = min(512, width_a)
        chunks = t_row // CHUNK

        def rotate(piece):
            def columns(j):
                at = rows_of(j, tile)
                aown[p, :, at] = jnp.dot(
                    inputs_all[p, rows_of(piece, t_row), :], basis_a[0, :, at], preferred_element_type=F32
                )

            each(0, width_a // tile, columns)

        def step(k):
            piece = lax.rem(r + k, n_row)
            rotate(piece)

            def store(i, value):
                asend[p, k, rows_of(i, CHUNK), :] = value

            quantize(lambda i: aown[p, rows_of(i, CHUNK), :], store, put(asend_s, p, k), chunks, width_a)
            acopy(p, k, k, r).start()

        each(1, n_row, step)
        rotate(r)
        if p == 0:
            load(1, "a").start()

    def sum_acts(p):
        chunks = t_row // CHUNK

        def step(k):
            source = lax.rem(r + n_row - k, n_row)
            acopy(p, k, k, source).wait_recv()
            add_scaled(aown.at[p], arecv.at[p, source], arecv_s[p, source, 0:1, 0:1], chunks)

        each(1, n_row, step)

        def store(i, value):
            afin[p, rows_of(i, CHUNK), :] = value

        quantize(lambda i: aown[p, rows_of(i, CHUNK), :], store, put(afin_s, p), chunks, width_a)
        each(1, n_row, lambda k: act_gather(p, k, r).start())
        pltpu.make_async_copy(afin.at[p], outs[p][2].at[r], local.at[p, 6]).start()
        pltpu.make_async_copy(afin_s.at[p], outs[p][3].at[r], local.at[p, 7]).start()

    rotate_grads(0)
    forward_inputs(0)
    rotate_grads(1)
    forward_inputs(1)
    sum_x(0)
    rotate_acts(0)
    sum_z(0)
    sum_x(1)
    rotate_acts(1)
    sum_z(1)
    forward_gather(0)
    sum_acts(0)
    sum_acts(1)
    forward_gather(1)

    for p in (0, 1):
        for at, (src, dst) in enumerate(
            ((fin.at[p], outs[p][0].at[c]), (fin_s.at[p], outs[p][1].at[c]),
             (afin.at[p], outs[p][2].at[r]), (afin_s.at[p], outs[p][3].at[r]))
        ):
            pltpu.make_async_copy(src, dst, local.at[p, 4 + at]).wait()
        gather_copy(p, 0, z * 2 + 1 - x, partner).wait_recv()

        def arrivals(k):
            gather_forward(p, k, lax.rem(z + nz - k, nz) * 2 + 1 - x).wait_recv()
            gather_forward(p, k, lax.rem(z + nz - k, nz) * 2 + x).wait_send()
            inputs_forward(p, k, lax.rem(z + nz - k, nz) * 2 + x).wait_send()
            inputs_copy(p, k, c, zpeer(k)).wait_send()
            gather_copy(p, k, c, zpeer(k)).wait_send()
            zcopy(p, k, lax.rem(z + k, nz), z).wait_send()

        each(1, nz, arrivals)

        def row_arrivals(k):
            act_gather(p, k, lax.rem(r + n_row - k, n_row)).wait_recv()
            act_gather(p, k, r).wait_send()
            acopy(p, k, k, r).wait_send()
            grads_copy(p, k, r).wait_send()

        each(1, n_row, row_arrivals)
        each(0, nz, lambda zz: xcopy(p, zz).wait_send())
        inputs_copy(p, 0, c, partner).wait_send()
        gather_copy(p, 0, c, partner).wait_send()


def rotate(n_row, n_col, query, output):
    inputs, grads, act_basis, grad_basis = query
    t_col, feats_a = inputs.shape
    t_row, feats_g = grads.shape
    width_a, width_g = act_basis.shape[1], grad_basis.shape[1]
    tokens, nz = t_col * n_col, n_col // 2
    one = (
        jax.ShapeDtypeStruct((n_col, t_col, width_g), I16),
        jax.ShapeDtypeStruct((n_col, 8, 128), F32),
        jax.ShapeDtypeStruct((n_row, t_row, width_a), I16),
        jax.ShapeDtypeStruct((n_row, 8, 128), F32),
    )
    dma = pltpu.SemaphoreType.DMA
    flops = 4 * tokens * (feats_a * width_a + feats_g * width_g)
    results = pl.pallas_call(
        functools.partial(rotate_kernel, n_row, n_col),
        out_shape=one + one,
        in_specs=[pl.BlockSpec(memory_space=pl.ANY)] * 8,
        out_specs=[pl.BlockSpec(memory_space=pl.ANY)] * 8,
        scratch_shapes=[
            pltpu.VMEM((2, tokens, feats_g), BF16),
            pltpu.VMEM((2, tokens, feats_a), BF16),
            pltpu.VMEM((2, feats_g, width_g), BF16),
            pltpu.VMEM((1, feats_a, width_a), BF16),
            pltpu.VMEM((2 * t_col, width_g), F32),
            pltpu.VMEM((2, nz, t_col, width_g), F32),
            pltpu.VMEM((2, nz, t_col, width_g), I16),
            pltpu.VMEM((2, nz, 8, 128), F32),
            pltpu.VMEM((2, nz, t_col, width_g), I16),
            pltpu.VMEM((2, nz, 8, 128), F32),
            pltpu.VMEM((2, nz, t_col, width_g), I16),
            pltpu.VMEM((2, nz, 8, 128), F32),
            pltpu.VMEM((2, t_col, width_g), I16),
            pltpu.VMEM((2, 8, 128), F32),
            pltpu.VMEM((2, t_row, width_a), F32),
            pltpu.VMEM((2, n_row, t_row, width_a), I16),
            pltpu.VMEM((2, n_row, 8, 128), F32),
            pltpu.VMEM((2, n_row, t_row, width_a), I16),
            pltpu.VMEM((2, n_row, 8, 128), F32),
            pltpu.VMEM((2, t_row, width_a), I16),
            pltpu.VMEM((2, 8, 128), F32),
            dma((2, n_row)), dma((2, n_row)),
            dma((2, nz)), dma((2, nz)), dma((2, n_col)),
            dma((2, nz, 2)), dma((2, nz, 2)), dma((2, nz, 2)), dma((2, nz, 2)),
            dma((2, nz, 2)), dma((2, nz, 2)), dma((2, n_col, 2)),
            dma((2, n_row, 2)), dma((2, n_row, 2)), dma((2, n_row, 2)), dma((2, n_row, 2)),
            dma((2, 8)),
        ],
        compiler_params=pltpu.CompilerParams(
            collective_id=0, has_side_effects=True, vmem_limit_bytes=62 * 2**20
        ),
        cost_estimate=pl.CostEstimate(flops=flops, bytes_accessed=32 * 2**20, transcendentals=0),
        name="rotate",
    )(*query, *output)
    return results[:4], results[4:]


def product_kernel(depth, starts, g_ref, gs_ref, a_ref, as_ref, out_ref, a_cat, g_raw, acc):
    blocks = a_ref.shape[0] // depth

    @pl.when(pl.program_id(0) == 0)
    def _():
        for b in range(blocks):
            at = pl.ds(b * depth, depth)
            value = widen(a_ref[at, :], as_ref[at, :])
            high = value.astype(BF16)
            low = (value - high.astype(F32)).astype(BF16)
            a_cat[b, pl.ds(0, depth), :] = high
            a_cat[b, pl.ds(depth, depth), :] = low
            a_cat[b, pl.ds(2 * depth, depth), :] = high

    for b in range(blocks):
        at = pl.ds(b * depth, depth)
        g_raw[b] = widen(g_ref[at, :], gs_ref[at, :])

    for s in range(SEQS):
        low_token, high_token = starts[s], starts[s + 1]
        acc[...] = jnp.zeros_like(acc)
        for b in range(blocks):

            @pl.when((low_token < (b + 1) * depth) & (high_token > b * depth))
            def _():
                place = lax.broadcasted_iota(I32, (depth, 1), 0) + b * depth
                value = jnp.where((place >= low_token) & (place < high_token), g_raw[b], 0.0)
                high = value.astype(BF16)
                low = (value - high.astype(F32)).astype(BF16)
                both = jnp.concatenate([high, high, low], axis=0)
                acc[...] += lax.dot_general(
                    both, a_cat[b], (((0,), (0,)), ((), ())), preferred_element_type=F32
                )

        if s == 0:
            out_ref[...] = acc[...] * acc[...]
        elif s < SEQS - 1:
            out_ref[...] += acc[...] * acc[...]
        else:
            out_ref[...] = (out_ref[...] + acc[...] * acc[...]) * (1.0 / SEQS)


def correct(starts, g, g_scale, a, a_scale):
    tokens = g.shape[0] * g.shape[1]
    gs = jnp.repeat(g_scale[:, 0, 0], g.shape[1])[:, None]
    acts = jnp.repeat(a_scale[:, 0, 0], a.shape[1])[:, None]
    g, a = g.reshape(tokens, -1), a.reshape(tokens, -1)
    width_g, width_a = g.shape[1], a.shape[1]
    depth, tile = min(256, tokens), min(512, width_g)
    blocks = tokens // depth
    return pl.pallas_call(
        functools.partial(product_kernel, depth),
        out_shape=jax.ShapeDtypeStruct((width_g, width_a), F32),
        grid_spec=pltpu.PrefetchScalarGridSpec(
            num_scalar_prefetch=1,
            grid=(width_g // tile,),
            in_specs=[
                pl.BlockSpec((tokens, tile), lambda i, s: (0, i)),
                pl.BlockSpec((tokens, 1), lambda i, s: (0, 0)),
                pl.BlockSpec((tokens, width_a), lambda i, s: (0, 0)),
                pl.BlockSpec((tokens, 1), lambda i, s: (0, 0)),
            ],
            out_specs=pl.BlockSpec((tile, width_a), lambda i, s: (i, 0)),
            scratch_shapes=[
                pltpu.VMEM((blocks, 3 * depth, width_a), BF16),
                pltpu.VMEM((blocks, depth, tile), F32),
                pltpu.VMEM((tile, width_a), F32),
            ],
        ),
        compiler_params=pltpu.CompilerParams(vmem_limit_bytes=56 * 2**20),
        cost_estimate=pl.CostEstimate(
            flops=2 * 6 * 7 * depth * width_g * width_a // 2, bytes_accessed=16 * 2**20, transcendentals=0
        ),
        name="correct",
    )(starts, g, gs, a, acts)


def per_device(n_row, n_col, seq_ids, *args):
    bounds = jnp.arange(SEQS + 1, dtype=I32)
    starts = jnp.sum((seq_ids[None, :] < bounds[:, None]).astype(I32), axis=1)
    query, output = rotate(n_row, n_col, args[:4], args[4:])
    return correct(starts, *query), correct(starts, *output)


def solution(mesh):
    one = (P("col", "row"), P("row", "col"), P("row", "col"), P("col", "row"))
    return jax.shard_map(
        functools.partial(per_device, mesh.shape["row"], mesh.shape["col"]),
        mesh=mesh,
        in_specs=(P(),) + one + one,
        out_specs=(P("row", "col"), P("row", "col")),
        check_vma=False,
    )
```

time: 1040 us -> 401 us (0.39)
  waiting for transfers between devices: 812 us -> 0 us
  Pallas kernels: 0 us -> 388 us
  matrix products: 188 us -> 0 us
  between operations: 22.3 us -> 0.64 us
    psum x2 -> x0, waiting for transfers between devices: 645 us -> none  [the longest x1 513 us: reduce_grad(): return lax.psum(partial_value, 'col')]
    pallas_call x0 -> x3, Pallas kernels: none -> 388 us  [the longest x1 316 us: rotate(): pl.pallas_call(functools.partial(rotate_kernel, n_row, n_col), out_shape=...]
    dot_general x12 -> x0, matrix products: 188 us -> none  [the longest x8 146 us: correct(): lax.dot_general(grad_rows, act_rows, (((0,), (0,)), ((), ())), precision=...]
    all_gather x4 -> x0, waiting for transfers between devices: 164 us -> none  [the longest x2 137 us: gather_act(): return lax.all_gather(inputs_now, 'col', axis=0, tiled=True)]
  transfers between devices with their start and end apart: 6 -> 0, of which waited for: 6 -> 0; matrix products, arithmetic and copies ran while one was open for 4% -> 0% of each run, Pallas kernels for 0% -> 0%
where the time goes in v1:
time: 401 us; the launch traced here: 396 us
  Pallas kernels  388 us (97%)
  local copies, waits for them, and re-layouts  6.25 us (2%)
    pallas_call x1, Pallas kernels, rotate(): pl.pallas_call(functools.partial(rotate_kernel, n_row, n_col), out_shape=...  316 us
    pallas_call x2, Pallas kernels, correct(): pl.pallas_call(functools.partial(product_kernel, depth), out_shape=jax.Sh...  71.6 us

profile of v1, /device:TPU:24, one launch (start us, length us, event | category | flops | bytes accessed | tf_op | source)
XLA Modules:
  0.0 396.2 jit_solution(397915690568852641)
XLA Ops:
  0.6 1.3 convert_reduce_fusion.starts
  2.0 316.4 %rotate.1 = (s16[8,128,2048]{2,1,0:T(8,128)(2,1)}, f32[8,8,128]{2,1,0:T(8,128)}, s16[4,256,1024]{2,1,0:T(8,128)(2,1)}, f32[4,8,128]{2,1,0:T(8,128)}, s16[8,128,2...) custom-call(bf16[128,2048]{1,0:T(8,128)(2,1)} %refs_0_.1, ...), custom_call_target="tpu_custom_call" | custom-call | flops 17179869184 | bytes 33554432 | tf_op jit(solution)/shard_map/rotate/pallas_call | solution.py:360
  318.4 0.9 slice_reduce_fusion
  319.3 0.9 slice_reduce_fusion.2
  320.1 0.1 broadcast_bitcast_fusion
  320.2 0.1 broadcast_in_dim.16
  320.3 0.1 broadcast_bitcast_fusion.1
  320.4 0.1 broadcast_in_dim.14
  320.4 1.1 copy.15.gs_ref
  321.5 1.1 copy.20
  322.6 1.0 copy.17.gs_ref
  323.6 1.0 copy.22
  324.6 35.8 %correct.3 = f32[2048,1024]{1,0:T(8,128)} custom-call(s32[5]{0:T(128)} %convert_reduce_fusion.starts, s16[1024,2048]{1,0:T(8,128)(2,1)} %bitcast.23, f32[1024,1]{1,0:T(8,128)} %copy.17.gs_ref, s16[1024,1024]{1,0:T(8,128)(2,1)} %bitcast.25, f32[1024,1]{1,0:T(8,128)} %bitcast.17), custom_call_target="tpu_custom_call" | custom-call | flops 22548578304 | bytes 16777216 | tf_op jit(solution)/shard_map/correct/pallas_call | solution.py:453
  360.4 35.8 %correct.2 = f32[2048,1024]{1,0:T(8,128)} custom-call(s32[5]{0:T(128)} %convert_reduce_fusion.starts, s16[1024,2048]{1,0:T(8,128)(2,1)} %bitcast.22, f32[1024,1]{1,0:T(8,128)} %copy.15.gs_ref, s16[1024,1024]{1,0:T(8,128)(2,1)} %bitcast.24, f32[1024,1]{1,0:T(8,128)} %bitcast.16), custom_call_target="tpu_custom_call" | custom-call | flops 22548578304 | bytes 16777216 | tf_op jit(solution)/shard_map/correct/pallas_call | solution.py:453
  (2 shorter events, 0.0 us)

commit v2 on v1

v2 whole, which is shorter than its diff:
```python
import functools

import jax
import jax.numpy as jnp
from jax import lax
from jax.experimental import pallas as pl
from jax.experimental.pallas import tpu as pltpu
from jax.sharding import PartitionSpec as P

SEQS = 4
CHUNK = 16
TOP = 32767.0
MESH = pl.DeviceIdType.MESH
F32, BF16, I16, I32 = jnp.float32, jnp.bfloat16, jnp.int16, jnp.int32


def quantize(load, store, store_scale, chunks, width):
    most = lax.fori_loop(
        0, chunks, lambda i, m: jnp.maximum(m, jnp.abs(load(i))), jnp.zeros((CHUNK, width), F32)
    )
    most = jnp.max(jnp.max(most, axis=1, keepdims=True), axis=0, keepdims=True)
    inverse = jnp.where(most > 1e-30, TOP / jnp.maximum(most, 1e-30), 0.0)
    store_scale(jnp.broadcast_to(most * (1.0 / TOP), (8, 128)))

    def body(i, carry):
        store(i, jnp.round(load(i) * inverse).astype(I32).astype(I16))
        return carry

    lax.fori_loop(0, chunks, body, 0)


def widen(codes, scale):
    return codes.astype(I32).astype(F32) * scale


def rows_of(i, size):
    return pl.ds(pl.multiple_of(i * size, size), size)


def rotate_kernel(n_row, n_col, depth, tile_g, parts, marks, flags, masks, *refs):
    ins, refs = (refs[0:4], refs[4:8]), refs[8:]
    outs, refs = (refs[0:5], refs[5:10]), refs[10:]
    (grads_all, inputs_all, basis_g, basis_a, block, own, xsend, xsend_s, xrecv, xrecv_s, zrecv, zrecv_s,
     fin, fin_s, aown, asend, asend_s, arecv, arecv_s, afin, afin_s,
     codes, codes_s, turned, acc, stage,
     g_send, g_recv, i_send, f_send, i_recv, xs_send, xs_recv, zs_send, zs_recv,
     ag_send, agf_send, ag_recv, as_send, as_recv, aa_send, aa_recv, local, codes_sem, stage_sem) = refs

    r, c = lax.axis_index("row"), lax.axis_index("col")
    nz = n_col // 2
    z, x = c // 2, lax.rem(c, 2)
    partner = (r, z * 2 + 1 - x)
    tokens = grads_all.shape[1] * grads_all.shape[2]
    feats_a = basis_a.shape[1]
    width_g, width_a = basis_g.shape[2], basis_a.shape[2]
    t_col, t_row = tokens // n_col, tokens // n_row

    def zpeer(k):
        return (r, lax.rem(z + k, nz) * 2 + x)

    def rpeer(k):
        return (lax.rem(r + k, n_row), c)

    def rdma(src, dst, send, recv, device):
        return pltpu.make_async_remote_copy(
            src_ref=src, dst_ref=dst, send_sem=send, recv_sem=recv, device_id=device, device_id_type=MESH
        )

    class pair:
        def __init__(self, src, src_s, dst, dst_s, send, recv, device):
            self.both = (
                rdma(src, dst, send.at[0], recv.at[0], device),
                rdma(src_s, dst_s, send.at[1], recv.at[1], device),
            )

        def start(self):
            for one in self.both:
                one.start()

        def wait_send(self):
            for one in self.both:
                one.wait_send()

        def wait_recv(self):
            for one in self.both:
                one.wait_recv()

    def each(low, high, body):
        lax.fori_loop(low, high, lambda i, carry: (body(i), carry)[1], 0)

    barrier = pltpu.get_barrier_semaphore()

    def greet(device):
        pl.semaphore_signal(barrier, inc=1, device_id=device, device_id_type=MESH)

    greet(partner)
    each(1, nz, lambda k: greet(zpeer(k)))
    each(1, n_row, lambda k: greet(rpeer(k)))
    pl.semaphore_wait(barrier, 1 + (nz - 1) + (n_row - 1))

    def place(i, size):
        runs = depth // size
        return lax.div(i, runs), rows_of(lax.rem(i, runs), size)

    def load(p, kind):
        if kind == "g":
            return pltpu.make_async_copy(ins[p][3], basis_g.at[0], local.at[p, 0])
        if kind == "a":
            return pltpu.make_async_copy(ins[p][2], basis_a.at[0], local.at[p, 1])
        if kind == "inputs":
            return pltpu.make_async_copy(ins[p][0], inputs_all.at[p, rows_of(c, t_col)], local.at[p, 2])
        return pltpu.make_async_copy(ins[p][1], grads_all.at[p, *place(r, t_row)], local.at[p, 3])

    def grads_copy(p, k, source):
        return rdma(ins[p][1], grads_all.at[p, *place(source, t_row)], g_send.at[p, k], g_recv.at[p, source], rpeer(k))

    def inputs_copy(p, k, source, device):
        return rdma(ins[p][0], inputs_all.at[p, rows_of(source, t_col)], i_send.at[p, k], i_recv.at[p, source], device)

    def inputs_forward(p, k, source):
        there = inputs_all.at[p, rows_of(source, t_col)]
        return rdma(there, there, f_send.at[p, k], i_recv.at[p, source], partner)

    def start_grads(p):
        load(p, "grads").start()
        each(1, n_row, lambda k: grads_copy(p, k, r).start())

    def start_inputs(p):
        load(p, "inputs").start()
        inputs_copy(p, 0, c, partner).start()
        each(1, nz, lambda k: inputs_copy(p, k, c, zpeer(k)).start())

    start_grads(0)
    start_inputs(0)
    load(0, "g").start()
    load(0, "a").start()

    def xcopy(p, zz):
        return pair(xsend.at[p, zz], xsend_s.at[p, zz], xrecv.at[p, zz], xrecv_s.at[p, zz],
                    xs_send.at[p, zz], xs_recv.at[p, zz], partner)

    def zcopy(p, k, slot):
        return pair(xrecv.at[p, slot], xrecv_s.at[p, slot], zrecv.at[p, k - 1], zrecv_s.at[p, k - 1],
                    zs_send.at[p, k], zs_recv.at[p, k], zpeer(k))

    part = width_g // parts

    def columns_of(q):
        return pl.ds(pl.multiple_of(q * part, part), part)

    def gather_copy(p, q, k, source, device):
        return rdma(fin.at[p, :, columns_of(q)], outs[p][0].at[source, :, columns_of(q)],
                    ag_send.at[p, k, q], ag_recv.at[p, source, q], device)

    def gather_forward(p, q, k, source):
        there = outs[p][0].at[source, :, columns_of(q)]
        return rdma(there, there, agf_send.at[p, k, q], ag_recv.at[p, source, q], partner)

    def scale_copy(p, k, source, device):
        return rdma(fin_s.at[p], outs[p][1].at[source], ag_send.at[p, k, parts], ag_recv.at[p, source, parts], device)

    def scale_forward(p, k, source):
        there = outs[p][1].at[source]
        return rdma(there, there, agf_send.at[p, k, parts], ag_recv.at[p, source, parts], partner)

    def acopy(p, k, slot, source):
        return pair(asend.at[p, slot], asend_s.at[p, slot], arecv.at[p, source], arecv_s.at[p, source],
                    as_send.at[p, k], as_recv.at[p, source], rpeer(k))

    def act_gather(p, k, source):
        return pair(afin.at[p], afin_s.at[p], outs[p][2].at[source], outs[p][3].at[source],
                    aa_send.at[p, k], aa_recv.at[p, source], rpeer(k))

    def put(ref, *at):
        def store(value):
            ref[at] = value

        return store

    def rotate_grads(p):
        load(p, "grads").wait()
        load(p, "g").wait()
        each(1, n_row, lambda k: grads_copy(p, k, lax.rem(r + n_row - k, n_row)).wait_recv())
        if p == 0:
            start_grads(1)
        tile = min(512, width_g)

        def step(k):
            zz = lax.rem(z + k, nz)

            def columns(j):
                at = rows_of(j, tile)
                block[:, at] = jnp.dot(
                    grads_all[p, *place(zz, 2 * t_col), :], basis_g[0, :, at], preferred_element_type=F32
                )

            each(0, width_g // tile, columns)
            there, here = (1 - x) * (t_col // CHUNK), x * (t_col // CHUNK)

            def store(i, value):
                xsend[p, zz, rows_of(i, CHUNK), :] = value

            quantize(lambda i: block[rows_of(there + i, CHUNK), :], store, put(xsend_s, p, zz),
                     t_col // CHUNK, width_g)
            xcopy(p, zz).start()

            def keep(i):
                own[p, zz, rows_of(i, CHUNK), :] = block[rows_of(here + i, CHUNK), :]

            each(0, t_col // CHUNK, keep)

        each(0, nz, step)
        if p == 0:
            load(1, "g").start()
            start_inputs(1)

    def forward_inputs(p):
        def step(k):
            source = lax.rem(z + nz - k, nz) * 2 + x
            inputs_copy(p, k, source, partner).wait_recv()
            inputs_forward(p, k, source).start()

        each(1, nz, step)

    def add_scaled(target, codes, scale, chunks):
        def step(i):
            at = rows_of(i, CHUNK)
            target[at, :] = target[at, :] + widen(codes[at, :], scale)

        each(0, chunks, step)

    def sum_x(p):
        chunks = t_col // CHUNK

        def step(k):
            zz = lax.rem(z + k, nz)
            xcopy(p, zz).wait_recv()
            add_scaled(own.at[p, zz], xrecv.at[p, zz], xrecv_s[p, zz, 0:1, 0:1], chunks)

            def store(i, value):
                xrecv[p, zz, rows_of(i, CHUNK), :] = value

            quantize(lambda i: own[p, zz, rows_of(i, CHUNK), :], store, put(xrecv_s, p, zz), chunks, width_g)
            zcopy(p, k, zz).start()

        each(1, nz, step)
        xcopy(p, z).wait_recv()
        add_scaled(own.at[p, z], xrecv.at[p, z], xrecv_s[p, z, 0:1, 0:1], chunks)

    def sum_z(p):
        chunks = t_col // CHUNK

        def step(k):
            zcopy(p, k, z).wait_recv()
            add_scaled(own.at[p, z], zrecv.at[p, k - 1], zrecv_s[p, k - 1, 0:1, 0:1], chunks)

        each(1, nz, step)

        def store(i, value):
            fin[p, rows_of(i, CHUNK), :] = value

        quantize(lambda i: own[p, z, rows_of(i, CHUNK), :], store, put(fin_s, p), chunks, width_g)
        scale_copy(p, 0, c, partner).start()
        each(1, nz, lambda k: scale_copy(p, k, c, zpeer(k)).start())

        def push(q):
            each(1, nz, lambda k: gather_copy(p, q, k, c, zpeer(k)).start())
            gather_copy(p, q, 0, c, partner).start()

        each(0, parts, push)
        pltpu.make_async_copy(fin.at[p], outs[p][0].at[c], local.at[p, 4]).start()
        pltpu.make_async_copy(fin_s.at[p], outs[p][1].at[c], local.at[p, 5]).start()

    def forward_scales(p):
        def step(k):
            source = lax.rem(z + nz - k, nz) * 2 + x
            scale_copy(p, k, source, partner).wait_recv()
            scale_forward(p, k, source).start()

        each(1, nz, step)

    def forward_gather(p, q):
        def step(k):
            source = lax.rem(z + nz - k, nz) * 2 + x
            gather_copy(p, q, k, source, partner).wait_recv()
            gather_forward(p, q, k, source).start()

        each(1, nz, step)

    def rotate_acts(p):
        load(p, "inputs").wait()
        load(p, "a").wait()
        inputs_copy(p, 0, z * 2 + 1 - x, partner).wait_recv()
        each(1, nz, lambda k: inputs_forward(p, k, lax.rem(z + nz - k, nz) * 2 + 1 - x).wait_recv())
        tile = min(512, width_a)
        chunks = t_row // CHUNK

        def rotate(piece):
            def columns(j):
                at = rows_of(j, tile)
                aown[p, :, at] = jnp.dot(
                    inputs_all[p, rows_of(piece, t_row), :], basis_a[0, :, at], preferred_element_type=F32
                )

            each(0, width_a // tile, columns)

        def step(k):
            piece = lax.rem(r + k, n_row)
            rotate(piece)

            def store(i, value):
                asend[p, k - 1, rows_of(i, CHUNK), :] = value

            quantize(lambda i: aown[p, rows_of(i, CHUNK), :], store, put(asend_s, p, k - 1), chunks, width_a)
            acopy(p, k, k - 1, r).start()

        each(1, n_row, step)
        rotate(r)
        if p == 0:
            load(1, "a").start()

    def sum_acts(p):
        chunks = t_row // CHUNK

        def step(k):
            source = lax.rem(r + n_row - k, n_row)
            acopy(p, k, k - 1, source).wait_recv()
            add_scaled(aown.at[p], arecv.at[p, source], arecv_s[p, source, 0:1, 0:1], chunks)

        each(1, n_row, step)

        def store(i, value):
            afin[p, rows_of(i, CHUNK), :] = value

        quantize(lambda i: aown[p, rows_of(i, CHUNK), :], store, put(afin_s, p), chunks, width_a)
        each(1, n_row, lambda k: act_gather(p, k, r).start())
        pltpu.make_async_copy(afin.at[p], outs[p][2].at[r], local.at[p, 6]).start()
        pltpu.make_async_copy(afin_s.at[p], outs[p][3].at[r], local.at[p, 7]).start()

    def own_copies(p):
        return [
            pltpu.make_async_copy(src, dst, local.at[p, 4 + at])
            for at, (src, dst) in enumerate(
                ((fin.at[p], outs[p][0].at[c]), (fin_s.at[p], outs[p][1].at[c]),
                 (afin.at[p], outs[p][2].at[r]), (afin_s.at[p], outs[p][3].at[r]))
            )
        ]

    blocks, per_block = tokens // depth, depth // t_col

    def prepare(p):
        for one in own_copies(p):
            one.wait()
        each(1, n_row, lambda k: act_gather(p, k, lax.rem(r + n_row - k, n_row)).wait_recv())
        both = (
            pltpu.make_async_copy(outs[p][2], arecv.at[p], codes_sem.at[0]),
            pltpu.make_async_copy(outs[p][3], arecv_s.at[p], codes_sem.at[1]),
        )
        for one in both:
            one.start()
        for one in both:
            one.wait()

        def split(piece):
            def step(i):
                value = widen(arecv[p, piece, rows_of(i, CHUNK), :], arecv_s[p, piece, 0:1, 0:1])
                high = value.astype(BF16)
                block_of, rows = place(piece * (t_row // CHUNK) + i, CHUNK)
                grads_all[0, block_of, rows, :] = high
                grads_all[1, block_of, rows, :] = (value - high.astype(F32)).astype(BF16)

            each(0, t_row // CHUNK, step)

        each(0, n_row, split)

    def arrived_scales(p):
        scale_copy(p, 0, z * 2 + 1 - x, partner).wait_recv()
        each(1, nz, lambda k: scale_forward(p, k, lax.rem(z + nz - k, nz) * 2 + 1 - x).wait_recv())
        copy = pltpu.make_async_copy(outs[p][1], codes_s, codes_sem.at[1])
        copy.start()
        copy.wait()

    def arrived(p, q):
        gather_copy(p, q, 0, z * 2 + 1 - x, partner).wait_recv()
        each(1, nz, lambda k: gather_forward(p, q, k, lax.rem(z + nz - k, nz) * 2 + 1 - x).wait_recv())

    def write(p, j):
        slot = lax.rem(j, 2)
        return pltpu.make_async_copy(stage.at[slot], outs[p][4].at[rows_of(j, tile_g)], stage_sem.at[slot])

    def multiply(m):
        b = marks[m]
        inside = masks[m, 0:1, :].astype(BF16)
        high, low = turned[b, :, pl.ds(0, depth)] * inside, turned[b, :, pl.ds(depth, depth)] * inside
        a_high, a_low = grads_all[0, b], grads_all[1, b]
        return jnp.dot(
            jnp.concatenate([high, high, low], axis=1),
            jnp.concatenate([a_high, a_low, a_high], axis=0),
            preferred_element_type=F32,
        )

    def product(p, j):
        copy = pltpu.make_async_copy(outs[p][0].at[:, :, rows_of(j, tile_g)], codes, codes_sem.at[0])
        copy.start()
        copy.wait()
        for b in range(blocks):
            at = pl.ds(b * per_block, per_block)
            value = widen(codes[at], codes_s[at, 0:1, 0:1]).reshape(depth, tile_g)
            high = value.astype(BF16)
            turned[b, :, pl.ds(0, depth)] = high.T
            turned[b, :, pl.ds(depth, depth)] = (value - high.astype(F32)).astype(BF16).T

        @pl.when(j >= 2)
        def _():
            write(p, j - 2).wait()

        slot = lax.rem(j, 2)
        acc[...] = multiply(0)
        stage[slot] = acc[...] * acc[...] * flags[1, 0]

        def step(m):
            acc[...] = acc[...] * flags[0, m] + multiply(m)
            stage[slot] = stage[slot] + acc[...] * acc[...] * flags[1, m]

        each(1, marks.shape[0], step)
        write(p, j).start()

    tiles, per_part = width_g // tile_g, part // tile_g

    rotate_grads(0)
    forward_inputs(0)
    rotate_grads(1)
    sum_x(0)
    rotate_acts(0)
    forward_inputs(1)
    sum_z(0)
    sum_x(1)
    sum_acts(0)
    rotate_acts(1)
    forward_scales(0)
    each(0, parts, lambda q: forward_gather(0, q))
    sum_z(1)
    sum_acts(1)
    prepare(0)
    arrived_scales(0)
    forward_scales(1)

    def overlap(q):
        arrived(0, q)
        each(q * per_part, (q + 1) * per_part, lambda j: product(0, j))
        forward_gather(1, q)

    def last(q):
        arrived(1, q)
        each(q * per_part, (q + 1) * per_part, lambda j: product(1, j))

    def drain(p):
        for j in range(max(0, tiles - 2), tiles):
            write(p, j).wait()

    each(0, parts, overlap)
    drain(0)
    prepare(1)
    arrived_scales(1)
    each(0, parts, last)
    drain(1)

    for p in (0, 1):

        def departures(k):
            source = lax.rem(z + nz - k, nz) * 2 + x
            scale_forward(p, k, source).wait_send()
            scale_copy(p, k, c, zpeer(k)).wait_send()
            each(0, parts, lambda q: gather_forward(p, q, k, source).wait_send())
            each(0, parts, lambda q: gather_copy(p, q, k, c, zpeer(k)).wait_send())
            inputs_copy(p, k, c, zpeer(k)).wait_send()
            inputs_forward(p, k, source).wait_send()
            zcopy(p, k, lax.rem(z + k, nz)).wait_send()

        each(1, nz, departures)

        def row_departures(k):
            act_gather(p, k, r).wait_send()
            acopy(p, k, k - 1, r).wait_send()
            grads_copy(p, k, r).wait_send()

        each(1, n_row, row_departures)
        each(0, nz, lambda zz: xcopy(p, zz).wait_send())
        inputs_copy(p, 0, c, partner).wait_send()
        scale_copy(p, 0, c, partner).wait_send()
        each(0, parts, lambda q: gather_copy(p, q, 0, c, partner).wait_send())


def segments(seq_ids, tokens, depth):
    starts = jnp.sum((seq_ids[None, :] < jnp.arange(1, SEQS, dtype=I32)[:, None]).astype(I32), axis=1)
    cuts = jnp.sort(jnp.concatenate([starts, jnp.arange(depth, tokens, depth, dtype=I32)]))
    low = jnp.concatenate([jnp.zeros((1,), I32), cuts])
    high = jnp.concatenate([cuts, jnp.full((1,), tokens, I32)])
    block = jnp.minimum(low // depth, tokens // depth - 1)
    numbers = jnp.sum((starts[None, :] <= low[:, None]).astype(I32), axis=1)
    same = (numbers[1:] == numbers[:-1]).astype(F32)
    goes_on = jnp.concatenate([jnp.zeros((1,), F32), same])
    ends = jnp.concatenate([1.0 - same, jnp.ones((1,), F32)]) / SEQS
    tokens_of = block[:, None] * depth + jnp.arange(depth, dtype=I32)[None, :]
    inside = ((tokens_of >= low[:, None]) & (tokens_of < high[:, None])).astype(F32)
    return block, jnp.stack([goes_on, ends]), jnp.repeat(inside[:, None, :], 8, axis=1)


def rotate(n_row, n_col, seq_ids, query, output):
    inputs, grads, act_basis, grad_basis = query
    t_col, feats_a = inputs.shape
    t_row, feats_g = grads.shape
    width_a, width_g = act_basis.shape[1], grad_basis.shape[1]
    tokens, nz = t_col * n_col, n_col // 2
    one = (
        jax.ShapeDtypeStruct((n_col, t_col, width_g), I16),
        jax.ShapeDtypeStruct((n_col, 8, 128), F32),
        jax.ShapeDtypeStruct((n_row, t_row, width_a), I16),
        jax.ShapeDtypeStruct((n_row, 8, 128), F32),
        jax.ShapeDtypeStruct((width_g, width_a), F32),
    )
    depth, tile_g = min(256, tokens), min(256, width_g)
    parts = max(1, min(4, width_g // tile_g))
    marks, flags, masks = segments(seq_ids, tokens, depth)
    dma = pltpu.SemaphoreType.DMA
    flops = 4 * tokens * (feats_a * width_a + feats_g * width_g + 6 * width_g * width_a)
    results = pl.pallas_call(
        functools.partial(rotate_kernel, n_row, n_col, depth, tile_g, parts),
        out_shape=one + one,
        in_specs=[pl.BlockSpec(memory_space=pltpu.SMEM)] * 2
        + [pl.BlockSpec(memory_space=pltpu.VMEM)]
        + [pl.BlockSpec(memory_space=pl.ANY)] * 8,
        out_specs=[pl.BlockSpec(memory_space=pl.ANY)] * 10,
        scratch_shapes=[
            pltpu.VMEM((2, tokens // depth, depth, feats_g), BF16),
            pltpu.VMEM((2, tokens, feats_a), BF16),
            pltpu.VMEM((1, feats_g, width_g), BF16),
            pltpu.VMEM((1, feats_a, width_a), BF16),
            pltpu.VMEM((2 * t_col, width_g), F32),
            pltpu.VMEM((2, nz, t_col, width_g), F32),
            pltpu.VMEM((2, nz, t_col, width_g), I16),
            pltpu.VMEM((2, nz, 8, 128), F32),
            pltpu.VMEM((2, nz, t_col, width_g), I16),
            pltpu.VMEM((2, nz, 8, 128), F32),
            pltpu.VMEM((2, nz - 1, t_col, width_g), I16),
            pltpu.VMEM((2, nz - 1, 8, 128), F32),
            pltpu.VMEM((2, t_col, width_g), I16),
            pltpu.VMEM((2, 8, 128), F32),
            pltpu.VMEM((2, t_row, width_a), F32),
            pltpu.VMEM((2, n_row - 1, t_row, width_a), I16),
            pltpu.VMEM((2, n_row - 1, 8, 128), F32),
            pltpu.VMEM((2, n_row, t_row, width_a), I16),
            pltpu.VMEM((2, n_row, 8, 128), F32),
            pltpu.VMEM((2, t_row, width_a), I16),
            pltpu.VMEM((2, 8, 128), F32),
            pltpu.VMEM((n_col, t_col, tile_g), I16),
            pltpu.VMEM((n_col, 8, 128), F32),
            pltpu.VMEM((tokens // depth, tile_g, 2 * depth), BF16),
            pltpu.VMEM((tile_g, width_a), F32),
            pltpu.VMEM((2, tile_g, width_a), F32),
            dma((2, n_row)), dma((2, n_row)),
            dma((2, nz)), dma((2, nz)), dma((2, n_col)),
            dma((2, nz, 2)), dma((2, nz, 2)), dma((2, nz, 2)), dma((2, nz, 2)),
            dma((2, nz, parts + 1)), dma((2, nz, parts + 1)), dma((2, n_col, parts + 1)),
            dma((2, n_row, 2)), dma((2, n_row, 2)), dma((2, n_row, 2)), dma((2, n_row, 2)),
            dma((2, 8)), dma((2,)), dma((2,)),
        ],
        compiler_params=pltpu.CompilerParams(
            collective_id=0, has_side_effects=True, vmem_limit_bytes=62 * 2**20
        ),
        cost_estimate=pl.CostEstimate(flops=flops, bytes_accessed=32 * 2**20, transcendentals=0),
        name="rotate",
    )(marks, flags, masks, *query, *output)
    return results[4], results[9]


def per_device(n_row, n_col, seq_ids, *args):
    return rotate(n_row, n_col, seq_ids, args[:4], args[4:])


def solution(mesh):
    one = (P("col", "row"), P("row", "col"), P("row", "col"), P("col", "row"))
    return jax.shard_map(
        functools.partial(per_device, mesh.shape["row"], mesh.shape["col"]),
        mesh=mesh,
        in_specs=(P(),) + one + one,
        out_specs=(P("row", "col"), P("row", "col")),
        check_vma=False,
    )
```

time: 401 us -> 383 us (0.955)
  Pallas kernels: 388 us -> 365 us
  local copies, waits for them, and re-layouts: 6.25 us -> 12.6 us
    pallas_call x3 -> x1, Pallas kernels: 388 us -> 365 us  [rotate(): pl.pallas_call(functools.partial(rotate_kernel, n_row, n_col, depth, tile...]
    unnamed x6 -> x4, local copies, waits for them, and re-layouts: 2.25 us -> 12 us
where the time goes in v2:
time: 383 us; the launch traced here: 382 us
  Pallas kernels  365 us (95%)
  local copies, waits for them, and re-layouts  12.6 us (3%)
    pallas_call x1, Pallas kernels, rotate(): pl.pallas_call(functools.partial(rotate_kernel, n_row, n_col, depth, tile...  365 us
    unnamed x4, local copies, waits for them, and re-layouts  12 us

profile of v2, /device:TPU:24, one launch (start us, length us, event | category | flops | bytes accessed | tf_op | source)
XLA Modules:
  0.0 381.5 jit_solution(11894809537200048409)
XLA Ops:
  0.6 0.9 convert_reduce_fusion
  1.5 0.1 pad_add_fusion
  1.6 1.0 sort.15
  2.6 0.7 broadcast_multiply_fusion
  3.2 0.1 convert_reduce_fusion.1
  3.3 0.1 subtract_bitcast_fusion
  3.4 0.1 maximum_multiply_fusion
  3.5 0.1 maximum_bitcast_fusion
  3.5 0.6 pad_maximum_fusion.flags
  4.1 0.1 fusion.3
  4.2 0.6 reshape.105.masks
  4.8 364.7 %rotate.1 = (s16[8,128,2048]{2,1,0:T(8,128)(2,1)}, f32[8,8,128]{2,1,0:T(8,128)}, s16[4,256,1024]{2,1,0:T(8,128)(2,1)}, f32[4,8,128]{2,1,0:T(8,128)}, f32[2048,10...) custom-call(s32[7]{0:T(128)} %get-tuple-element.10.marks, ...), custom_call_target="tpu_custom_call" | custom-call | flops 68719476736 | bytes 33554432 | tf_op jit(solution)/shard_map/rotate/pallas_call | solution.py:527
  369.5 0.0 copy-start
  369.5 8.6 %copy.13 = f32[2048,1024]{1,0:T(8,128)} copy(f32[2048,1024]{1,0:T(8,128)} %get-tuple-element.17) | data formatting | bytes 16777216
  378.1 0.0 copy-done
  378.1 3.4 copy.14
  (3 shorter events, 0.0 us)
Async XLA Ops:
  369.5 8.6 %copy-start = (f32[2048,1024]{1,0:T(8,128)S(1)}, f32[2048,1024]{1,0:T(8,128)}, u32[]{:S(2)}) copy-start(f32[2048,1024]{1,0:T(8,128)} %get-tuple-element.18) | copy-start | bytes 25165828

commit v3 on v2

--- a/solution.py
+++ b/solution.py
@@ -41,7 +41,7 @@
     ins, refs = (refs[0:4], refs[4:8]), refs[8:]
     outs, refs = (refs[0:5], refs[5:10]), refs[10:]
     (grads_all, inputs_all, basis_g, basis_a, block, own, xsend, xsend_s, xrecv, xrecv_s, zrecv, zrecv_s,
-     fin, fin_s, aown, asend, asend_s, arecv, arecv_s, afin, afin_s,
+     fin_s, aown, asend, asend_s, arecv, arecv_s, afin, afin_s,
      codes, codes_s, turned, acc, stage,
      g_send, g_recv, i_send, f_send, i_recv, xs_send, xs_recv, zs_send, zs_recv,
      ag_send, agf_send, ag_recv, as_send, as_recv, aa_send, aa_recv, local, codes_sem, stage_sem) = refs
@@ -127,11 +127,12 @@
 
     def start_inputs(p):
         load(p, "inputs").start()
-        inputs_copy(p, 0, c, partner).start()
         each(1, nz, lambda k: inputs_copy(p, k, c, zpeer(k)).start())
 
     start_grads(0)
     start_inputs(0)
+    inputs_copy(0, 0, c, partner).start()
+    inputs_copy(1, 0, c, partner).start()
     load(0, "g").start()
     load(0, "a").start()
 
@@ -149,7 +150,7 @@
         return pl.ds(pl.multiple_of(q * part, part), part)
 
     def gather_copy(p, q, k, source, device):
-        return rdma(fin.at[p, :, columns_of(q)], outs[p][0].at[source, :, columns_of(q)],
+        return rdma(xrecv.at[p, z, :, columns_of(q)], outs[p][0].at[source, :, columns_of(q)],
                     ag_send.at[p, k, q], ag_recv.at[p, source, q], device)
 
     def gather_forward(p, q, k, source):
@@ -257,7 +258,7 @@
         each(1, nz, step)
 
         def store(i, value):
-            fin[p, rows_of(i, CHUNK), :] = value
+            xrecv[p, z, rows_of(i, CHUNK), :] = value
 
         quantize(lambda i: own[p, z, rows_of(i, CHUNK), :], store, put(fin_s, p), chunks, width_g)
         scale_copy(p, 0, c, partner).start()
@@ -268,7 +269,7 @@
             gather_copy(p, q, 0, c, partner).start()
 
         each(0, parts, push)
-        pltpu.make_async_copy(fin.at[p], outs[p][0].at[c], local.at[p, 4]).start()
+        pltpu.make_async_copy(xrecv.at[p, z], outs[p][0].at[c], local.at[p, 4]).start()
         pltpu.make_async_copy(fin_s.at[p], outs[p][1].at[c], local.at[p, 5]).start()
 
     def forward_scales(p):
@@ -341,7 +342,7 @@
         return [
             pltpu.make_async_copy(src, dst, local.at[p, 4 + at])
             for at, (src, dst) in enumerate(
-                ((fin.at[p], outs[p][0].at[c]), (fin_s.at[p], outs[p][1].at[c]),
+                ((xrecv.at[p, z], outs[p][0].at[c]), (fin_s.at[p], outs[p][1].at[c]),
                  (afin.at[p], outs[p][2].at[r]), (afin_s.at[p], outs[p][3].at[r]))
             )
         ]
@@ -385,19 +386,23 @@
         each(1, nz, lambda k: gather_forward(p, q, k, lax.rem(z + nz - k, nz) * 2 + 1 - x).wait_recv())
 
     def write(p, j):
-        slot = lax.rem(j, 2)
-        return pltpu.make_async_copy(stage.at[slot], outs[p][4].at[rows_of(j, tile_g)], stage_sem.at[slot])
+        return pltpu.make_async_copy(stage, outs[p][4].at[rows_of(j, tile_g)], stage_sem.at[0])
+
+    strip = min(512, width_a)
+    strips = [pl.ds(n * strip, strip) for n in range(width_a // strip)]
 
     def multiply(m):
         b = marks[m]
         inside = masks[m, 0:1, :].astype(BF16)
         high, low = turned[b, :, pl.ds(0, depth)] * inside, turned[b, :, pl.ds(depth, depth)] * inside
-        a_high, a_low = grads_all[0, b], grads_all[1, b]
-        return jnp.dot(
-            jnp.concatenate([high, high, low], axis=1),
-            jnp.concatenate([a_high, a_low, a_high], axis=0),
-            preferred_element_type=F32,
-        )
+        left = jnp.concatenate([high, high, low], axis=1)
+
+        def part_of(at):
+            a_high, a_low = grads_all[0, b, :, at], grads_all[1, b, :, at]
+            right = jnp.concatenate([a_high, a_low, a_high], axis=0)
+            return jnp.dot(left, right, preferred_element_type=F32)
+
+        return part_of
 
     def product(p, j):
         copy = pltpu.make_async_copy(outs[p][0].at[:, :, rows_of(j, tile_g)], codes, codes_sem.at[0])
@@ -410,17 +415,22 @@
             turned[b, :, pl.ds(0, depth)] = high.T
             turned[b, :, pl.ds(depth, depth)] = (value - high.astype(F32)).astype(BF16).T
 
-        @pl.when(j >= 2)
+        @pl.when(j >= 1)
         def _():
-            write(p, j - 2).wait()
-
-        slot = lax.rem(j, 2)
-        acc[...] = multiply(0)
-        stage[slot] = acc[...] * acc[...] * flags[1, 0]
+            write(p, j - 1).wait()
+
+        part_of = multiply(0)
+        for at in strips:
+            total = part_of(at)
+            acc[:, at] = total
+            stage[:, at] = total * total * flags[1, 0]
 
         def step(m):
-            acc[...] = acc[...] * flags[0, m] + multiply(m)
-            stage[slot] = stage[slot] + acc[...] * acc[...] * flags[1, m]
+            part_of = multiply(m)
+            for at in strips:
+                total = acc[:, at] * flags[0, m] + part_of(at)
+                acc[:, at] = total
+                stage[:, at] = stage[:, at] + total * total * flags[1, m]
 
         each(1, marks.shape[0], step)
         write(p, j).start()
@@ -431,19 +441,19 @@
     forward_inputs(0)
     rotate_grads(1)
     sum_x(0)
+    forward_inputs(1)
     rotate_acts(0)
-    forward_inputs(1)
     sum_z(0)
     sum_x(1)
     sum_acts(0)
+    forward_scales(0)
+    prepare(0)
     rotate_acts(1)
-    forward_scales(0)
     each(0, parts, lambda q: forward_gather(0, q))
     sum_z(1)
     sum_acts(1)
-    prepare(0)
+    forward_scales(1)
     arrived_scales(0)
-    forward_scales(1)
 
     def overlap(q):
         arrived(0, q)
@@ -455,8 +465,7 @@
         each(q * per_part, (q + 1) * per_part, lambda j: product(1, j))
 
     def drain(p):
-        for j in range(max(0, tiles - 2), tiles):
-            write(p, j).wait()
+        write(p, tiles - 1).wait()
 
     each(0, parts, overlap)
     drain(0)
@@ -519,7 +528,7 @@
         jax.ShapeDtypeStruct((n_row, 8, 128), F32),
         jax.ShapeDtypeStruct((width_g, width_a), F32),
     )
-    depth, tile_g = min(256, tokens), min(256, width_g)
+    depth, tile_g = min(256, tokens), min(512, width_g)
     parts = max(1, min(4, width_g // tile_g))
     marks, flags, masks = segments(seq_ids, tokens, depth)
     dma = pltpu.SemaphoreType.DMA
@@ -544,7 +553,6 @@
             pltpu.VMEM((2, nz, 8, 128), F32),
             pltpu.VMEM((2, nz - 1, t_col, width_g), I16),
             pltpu.VMEM((2, nz - 1, 8, 128), F32),
-            pltpu.VMEM((2, t_col, width_g), I16),
             pltpu.VMEM((2, 8, 128), F32),
             pltpu.VMEM((2, t_row, width_a), F32),
             pltpu.VMEM((2, n_row - 1, t_row, width_a), I16),
@@ -557,13 +565,13 @@
             pltpu.VMEM((n_col, 8, 128), F32),
             pltpu.VMEM((tokens // depth, tile_g, 2 * depth), BF16),
             pltpu.VMEM((tile_g, width_a), F32),
-            pltpu.VMEM((2, tile_g, width_a), F32),
+            pltpu.VMEM((tile_g, width_a), F32),
             dma((2, n_row)), dma((2, n_row)),
             dma((2, nz)), dma((2, nz)), dma((2, n_col)),
             dma((2, nz, 2)), dma((2, nz, 2)), dma((2, nz, 2)), dma((2, nz, 2)),
             dma((2, nz, parts + 1)), dma((2, nz, parts + 1)), dma((2, n_col, parts + 1)),
             dma((2, n_row, 2)), dma((2, n_row, 2)), dma((2, n_row, 2)), dma((2, n_row, 2)),
-            dma((2, 8)), dma((2,)), dma((2,)),
+            dma((2, 8)), dma((2,)), dma((1,)),
         ],
         compiler_params=pltpu.CompilerParams(
             collective_id=0, has_side_effects=True, vmem_limit_bytes=62 * 2**20

time: 383 us -> 363 us (0.948); the launches traced: 382 us -> 358 us
  Pallas kernels: 365 us -> 341 us
    pallas_call x1, Pallas kernels: 365 us -> 341 us  [rotate(): pl.pallas_call(functools.partial(rotate_kernel, n_row, n_col, depth, tile...]
where the time goes in v3:
time: 363 us; the launch traced here: 358 us
  Pallas kernels  341 us (94%)
  local copies, waits for them, and re-layouts  12.6 us (3%)
    pallas_call x1, Pallas kernels, rotate(): pl.pallas_call(functools.partial(rotate_kernel, n_row, n_col, depth, tile...  341 us
    unnamed x4, local copies, waits for them, and re-layouts  12 us

profile of v3, /device:TPU:24, one launch (start us, length us, event | category | flops | bytes accessed | tf_op | source)
XLA Modules:
  0.0 357.5 jit_solution(18403626917112049015)
XLA Ops:
  0.6 0.9 convert_reduce_fusion
  1.5 0.1 pad_add_fusion
  1.6 1.0 sort.15
  2.6 0.7 broadcast_multiply_fusion
  3.2 0.1 convert_reduce_fusion.1
  3.3 0.1 subtract_bitcast_fusion
  3.4 0.1 maximum_multiply_fusion
  3.5 0.1 maximum_bitcast_fusion
  3.5 0.6 pad_maximum_fusion.flags
  4.1 0.1 fusion.3
  4.2 0.6 reshape.105.masks
  4.8 340.7 %rotate.1 = (s16[8,128,2048]{2,1,0:T(8,128)(2,1)}, f32[8,8,128]{2,1,0:T(8,128)}, s16[4,256,1024]{2,1,0:T(8,128)(2,1)}, f32[4,8,128]{2,1,0:T(8,128)}, f32[2048,10...) custom-call(s32[7]{0:T(128)} %get-tuple-element.10.marks, ...), custom_call_target="tpu_custom_call" | custom-call | flops 68719476736 | bytes 33554432 | tf_op jit(solution)/shard_map/rotate/pallas_call | solution.py:536
  345.5 0.0 copy-start
  345.5 8.6 %copy.13 = f32[2048,1024]{1,0:T(8,128)} copy(f32[2048,1024]{1,0:T(8,128)} %get-tuple-element.17) | data formatting | bytes 16777216
  354.1 0.0 copy-done
  354.1 3.4 copy.14
  (3 shorter events, 0.0 us)
Async XLA Ops:
  345.5 8.6 %copy-start = (f32[2048,1024]{1,0:T(8,128)S(1)}, f32[2048,1024]{1,0:T(8,128)}, u32[]{:S(2)}) copy-start(f32[2048,1024]{1,0:T(8,128)} %get-tuple-element.18) | copy-start | bytes 25165828

commit v4 on v3

--- a/solution.py
+++ b/solution.py
@@ -447,11 +447,11 @@
     sum_x(1)
     sum_acts(0)
     forward_scales(0)
-    prepare(0)
+    each(0, parts, lambda q: forward_gather(0, q))
     rotate_acts(1)
-    each(0, parts, lambda q: forward_gather(0, q))
     sum_z(1)
     sum_acts(1)
+    prepare(0)
     forward_scales(1)
     arrived_scales(0)
 

time: 363 us -> 365 us (level)
  Pallas kernels: 341 us -> 345 us
    pallas_call x1, Pallas kernels: 341 us -> 345 us  [rotate(): pl.pallas_call(functools.partial(rotate_kernel, n_row, n_col, depth, tile...]
where the time goes in v4:
time: 365 us; the launch traced here: 362 us
  Pallas kernels  345 us (95%)
  local copies, waits for them, and re-layouts  12.6 us (3%)
    pallas_call x1, Pallas kernels, rotate(): pl.pallas_call(functools.partial(rotate_kernel, n_row, n_col, depth, tile...  345 us
    unnamed x4, local copies, waits for them, and re-layouts  12 us

profile of v4, /device:TPU:24, one launch (start us, length us, event | category | flops | bytes accessed | tf_op | source)
XLA Modules:
  0.0 361.9 jit_solution(5200413446171595517)
XLA Ops:
  0.6 0.9 convert_reduce_fusion
  1.5 0.1 pad_add_fusion
  1.6 1.0 sort.15
  2.6 0.7 broadcast_multiply_fusion
  3.2 0.1 convert_reduce_fusion.1
  3.3 0.1 subtract_bitcast_fusion
  3.4 0.1 maximum_multiply_fusion
  3.5 0.1 maximum_bitcast_fusion
  3.5 0.6 pad_maximum_fusion.flags
  4.1 0.1 fusion.3
  4.2 0.6 reshape.105.masks
  4.8 345.1 %rotate.1 = (s16[8,128,2048]{2,1,0:T(8,128)(2,1)}, f32[8,8,128]{2,1,0:T(8,128)}, s16[4,256,1024]{2,1,0:T(8,128)(2,1)}, f32[4,8,128]{2,1,0:T(8,128)}, f32[2048,10...) custom-call(s32[7]{0:T(128)} %get-tuple-element.10.marks, ...), custom_call_target="tpu_custom_call" | custom-call | flops 68719476736 | bytes 33554432 | tf_op jit(solution)/shard_map/rotate/pallas_call | solution.py:536
  349.9 0.0 copy-start
  349.9 8.6 %copy.13 = f32[2048,1024]{1,0:T(8,128)} copy(f32[2048,1024]{1,0:T(8,128)} %get-tuple-element.17) | data formatting | bytes 16777216
  358.5 0.0 copy-done
  358.5 3.4 copy.14
  (3 shorter events, 0.0 us)
Async XLA Ops:
  349.9 8.6 %copy-start = (f32[2048,1024]{1,0:T(8,128)S(1)}, f32[2048,1024]{1,0:T(8,128)}, u32[]{:S(2)}) copy-start(f32[2048,1024]{1,0:T(8,128)} %get-tuple-element.18) | copy-start | bytes 25165828
